TPU v7x, 256 devices: a whole 4x4x8 slice. The times are simulated.
256 devices in a mesh: rows: 64 (over x, z, core), sub: 4 (over y).
Axes of the slice: x: 4, y: 4, z: 8, core: 2. Of those that a mesh axis runs over, the one named last changes fastest.
Arguments:
- a_tiles: bfloat16 [2560, 8, 128, 128], P(('rows', 'sub')), may hold values from -0.1875 to 0.1875
- a_cols: int32 [2560, 8], P(('rows', 'sub')), may hold values from 0 to 2559, as said below
- a_count: int32 [2560], P(('rows', 'sub')), may hold values from 4 to 8, as said below
- p_tiles: bfloat16 [2560, 3, 128, 128], P(('rows', 'sub')), may hold values from -1 to 1
- aggregate: int32 [256, 10], replicated, may hold values from 0 to 4, never falling along the last dimension, each value on 1 to 3 neighbouring positions
- rep_list: int32 [256, 2, 4], replicated, may hold values from 0 to 9, as said below
Outputs:
- coarse: bfloat16 [1280, 21, 128, 128], P(('rows', 'sub'))
Inputs may be any that keep to these rules, and one draw needn't show every extreme that they name: `a_cols`: each entry is a fine panel within 8 panels of its row panel; slot 0 is the row panel itself; the entries of a row panel are distinct; a panel of another device appears only if it is on that device's replication list toward this one. The live slots of a row panel are its first a_count slots; 8 is reached. `rep_list`: row 0 holds 4 distinct ascending indices among the device's first 8 panels, row 1 among its last 8. `aggregate`: along a device's panels never falling and rising by at most one; every coarse panel of a device has 1 to 3 fine panels, and 3 is reached.
All inputs are finite; a program needn't handle non-finite values.
Results may differ from a plain program's by a relative error of at most 0.0051.
Values may be sent and summed in bfloat16 or wider, within the bound.
A program may use at most 128 MiB of HBM per device.

v0:
```python
import jax
import jax.numpy as jnp
from jax import lax
from jax.sharding import PartitionSpec as P

REACH = 8
CP_DEV = 5


def with_halo(block, sides, width):
    for axis, dim in sides:
        count = lax.axis_size(axis)
        forward = [(i, i + 1) for i in range(count - 1)]
        backward = [(target, source) for source, target in forward]
        low = lax.ppermute(
            lax.slice_in_dim(block, block.shape[dim] - width, None, axis=dim), axis, forward
        )
        high = lax.ppermute(lax.slice_in_dim(block, 0, width, axis=dim), axis, backward)
        block = jnp.concatenate([low, block, high], axis=dim)
    return block


def shifted(block, axis, distance):
    devices = range(lax.axis_size(axis))
    route = [(i - distance, i) for i in devices if i - distance in devices]
    return lax.ppermute(block, axis, route)


def coarse_rows(dev, a_blk, cols, count, p_ext, aggregate, rep_list):
    fp = a_blk.shape[0]
    ka = a_blk.shape[1]
    pb = a_blk.shape[2]
    ndev = aggregate.shape[0]
    total = ndev * fp
    ncoarse = ndev * CP_DEV
    kw = 2 * REACH + 3
    kc = 2 * REACH + 5
    flat = aggregate.reshape(-1)
    base = dev * fp

    def coarse_of(index):
        held = jnp.clip(index, 0, total - 1)
        return held // fp * CP_DEV + flat[held]

    g_own = coarse_of(base + jnp.arange(fp, dtype=jnp.int32))
    g_col = coarse_of(cols)
    dev_col = jnp.clip(cols, 0, total - 1) // fp
    local_col = cols % fp
    side = jnp.where(dev_col > dev, 0, 1)
    listed = jnp.any(rep_list[dev_col, side, :] == local_col[:, :, None], axis=-1)
    live = (jnp.arange(ka, dtype=jnp.int32)[None, :] < count[:, None]) & ((dev_col == dev) | listed)
    shifts = jnp.arange(3, dtype=jnp.int32) - 1
    own_target = g_own[:, None] + shifts[None, :]
    own_live = ((own_target >= 0) & (own_target < ncoarse)).astype(jnp.bfloat16)
    col_target = g_col[:, :, None] + shifts[None, None, :]
    col_live = ((col_target >= 0) & (col_target < ncoarse)).astype(jnp.bfloat16)
    live_mask = live.astype(jnp.bfloat16)
    slot_base = g_col - g_own[:, None] + REACH
    lead = g_own - dev * CP_DEV
    ext_index = cols - base + REACH
    zero = jnp.zeros((), jnp.int32)

    def step(panel, acc):
        a_row = lax.dynamic_index_in_dim(a_blk, panel, 0, keepdims=False)
        a_row = a_row * lax.dynamic_index_in_dim(live_mask, panel, 0, keepdims=False)[:, None, None]
        picked = jnp.take(p_ext, ext_index[panel], axis=0)
        picked = (
            picked * lax.dynamic_index_in_dim(col_live, panel, 0, keepdims=False)[:, :, None, None]
        )
        prods = jnp.einsum("kab,kqbc->kqac", a_row, picked, preferred_element_type=jnp.float32)
        window = jnp.zeros((kw, pb, pb), jnp.float32)
        for slot_k in range(ka):
            where = slot_base[panel, slot_k]
            current = lax.dynamic_slice_in_dim(window, where, 3, 0)
            window = lax.dynamic_update_slice_in_dim(window, current + prods[slot_k], where, 0)
        product = window.astype(jnp.bfloat16)
        own_p = lax.dynamic_index_in_dim(p_ext, panel + REACH, 0, keepdims=False)
        own_p = own_p * lax.dynamic_index_in_dim(own_live, panel, 0, keepdims=False)[:, None, None]
        terms = jnp.einsum("qba,rbc->qrac", own_p, product, preferred_element_type=jnp.float32)
        for block in range(3):
            row = lead[panel] + block
            begin = (row, zero + (2 - block), zero, zero)
            current = lax.dynamic_slice(acc, begin, (1, kw, pb, pb))
            acc = lax.dynamic_update_slice(acc, current + terms[block][None], begin)
        return acc

    start = jnp.zeros((CP_DEV + 2, kc, pb, pb), jnp.float32)
    return lax.fori_loop(0, fp, step, start)


def body(a_tiles, a_cols, a_count, p_tiles, aggregate, rep_list):
    dev = lax.axis_index(("rows", "sub"))
    p_ext = with_halo(p_tiles, ((("rows", "sub"), 0),), REACH)
    acc = coarse_rows(dev, a_tiles, a_cols, a_count, p_ext, aggregate, rep_list)
    own = acc[1 : CP_DEV + 1]
    lower_part = acc[0].astype(jnp.bfloat16)
    upper_part = acc[CP_DEV + 1].astype(jnp.bfloat16)
    from_lower_dev = shifted(upper_part, ("rows", "sub"), 1)
    from_upper_dev = shifted(lower_part, ("rows", "sub"), -1)
    own = own.at[0].add(from_lower_dev.astype(jnp.float32))
    own = own.at[CP_DEV - 1].add(from_upper_dev.astype(jnp.float32))
    return own.astype(jnp.bfloat16)


def solution(mesh):
    in_specs = (
        P(("rows", "sub"), None, None, None),
        P(("rows", "sub"), None),
        P(("rows", "sub")),
        P(("rows", "sub"), None, None, None),
        P(),
        P(),
    )
    out_specs = P(("rows", "sub"), None, None, None)
    return jax.shard_map(body, mesh=mesh, in_specs=in_specs, out_specs=out_specs, check_vma=False)
```

profile of v0, /device:TPU:6, one launch (start us, length us, event | category | flops | bytes accessed | tf_op | source)
XLA Modules:
  0.0 502.2 jit_solution(716313653042626180)
XLA Ops:
  1.5 3.5 collective-permute-start
  5.0 8.4 %collective-permute-start.1 = (bf16[8,3,128,128]{3,2,1,0:T(8,128)(2,1)S(1)}, bf16[8,3,128,128]{3,2,1,0:T(8,128)(2,1)}, u32[]{:S(2)}, u32[]{:S(2)}) collective-permute-start(bf16[8,3,128,128]{3,2,1,0:T(8,128)(2,1)S(1)} %get-tuple-element.329), channel_id=1, source_target_pairs={{1,0},{2,1},{3,2},{4,3},{5,4},{6,5},{7,6},{8,7},{9,8},{10,9},{11,1... | collective-permute-start | bytes 2359304 | tf_op jit(solution)/shard_map/ppermute | solution.py:18
  18.0 3.7 collective-permute-done
  22.7 3.3 collective-permute-done.1
  28.0 4.9 broadcast_in_dim.60
  32.9 428.0 %while.17 = (s32[]{:T(128)}, f32[7,21,128,128]{2,3,0,1:T(8,128)}, s32[10]{0:T(128)S(1)}, s32[10,8]{1,0:T(8,128)S(1)}, bf16[26,3,128,128]{3,2,1,0:T(8,128)(2,1)S(...) while((s32[]{:T(128)}, f32[7,21,128,128]{2,3,0,1:T(8,128)}, ...), condition=%wide.region_2.3_spmd, body=%wide.region_1.2_spmd.sunk | while | flops 342443072 | bytes 52991796 | solution.py:88
  58.1 3.5 convolution_bitcast_fusion.5
  72.6 3.1 fusion.90
  100.9 3.5 convolution_bitcast_fusion.5
  115.3 3.1 fusion.90
  143.7 3.5 convolution_bitcast_fusion.5
  158.1 3.1 fusion.90
  186.5 3.5 convolution_bitcast_fusion.5
  201.0 3.1 fusion.90
  229.3 3.5 convolution_bitcast_fusion.5
  243.8 3.1 fusion.90
  272.1 3.5 convolution_bitcast_fusion.5
  286.6 3.1 fusion.90
  315.0 3.5 convolution_bitcast_fusion.5
  329.5 3.1 fusion.90
  357.8 3.5 convolution_bitcast_fusion.5
  372.3 3.0 fusion.90
  400.6 3.5 convolution_bitcast_fusion.5
  415.1 3.0 fusion.90
  443.4 3.5 convolution_bitcast_fusion.5
  457.8 3.0 fusion.90
  460.9 11.2 %copy.25 = f32[7,21,128,128]{3,2,1,0:T(8,128)} copy(f32[7,21,128,128]{2,3,0,1:T(8,128)} %get-tuple-element.273) | data formatting | bytes 19267584 | tf_op jit(solution)/shard_map/while | solution.py:88
  472.1 4.9 convert.10
  477.1 3.8 collective-permute-start.2
  481.0 6.5 %collective-permute-start.3 = (bf16[21,128,128]{2,1,0:T(8,128)(2,1)S(1)}, bf16[21,128,128]{2,1,0:T(8,128)(2,1)S(1)}, u32[]{:S(2)}, u32[]{:S(2)}) collective-permute-start(bf16[21,128,128]{2,1,0:T(8,128)(2,1)S(1)} %get-tuple-element.326), channel_id=1, source_target_pairs={{1,0},{2,1},{3,2},{4,3},{5,4},{6,5},{7,6},{8,7},{9,8},{10,9},{11,1... | collective-permute-start | bytes 2064392 | tf_op jit(solution)/shard_map/ppermute | solution.py:26
  487.5 7.0 %collective-permute-done.2 = bf16[21,128,128]{2,1,0:T(8,128)(2,1)S(1)} collective-permute-done((bf16[21,128,128]{2,1,0:T(8,128)(2,1)S(1)}, bf16[21,128,128]{2,1,0:T(8,128)(2,1)S(1)}, u32[]{:S(2)}, u32[]{:S(2)}) %collective-permute-start.2) | collective-permute-done | bytes 688160 | tf_op jit(solution)/shard_map/ppermute | solution.py:26
  494.7 4.7 collective-permute-done.3
  (322 shorter events, 183.0 us)
Async XLA Ops:
  0.0 13.4 %copy-start.5 = (s32[256,10]{0,1:T(8,128)S(1)}, s32[256,10]{0,1:T(8,128)}, u32[]{:S(2)}) copy-start(s32[256,10]{0,1:T(8,128)} %param.16) | copy-start | bytes 30724
  0.0 13.7 %copy-start.7 = (s32[10,8]{0,1:T(8,128)S(1)}, s32[10,8]{0,1:T(8,128)}, u32[]{:S(2)}) copy-start(s32[10,8]{0,1:T(8,128)} %param.13) | copy-start | bytes 964
  1.5 20.3 %collective-permute-start = (bf16[8,3,128,128]{3,2,1,0:T(8,128)(2,1)S(1)}, bf16[8,3,128,128]{3,2,1,0:T(8,128)(2,1)S(1)}, u32[]{:S(2)}, u32[]{:S(2)}) collective-permute-start(bf16[8,3,128,128]{3,2,1,0:T(8,128)(2,1)S(1)} %get-tuple-element.328), channel_id=1, source_target_pairs={{0,1},{1,2},{2,3},{3,4},{4,5},{5,6},{6,7},{7,8},{8,9},{9,10},{10,1... | collective-permute-start | bytes 2359304 | tf_op jit(solution)/shard_map/ppermute | solution.py:15
  5.0 21.0 %collective-permute-start.1 = (bf16[8,3,128,128]{3,2,1,0:T(8,128)(2,1)S(1)}, bf16[8,3,128,128]{3,2,1,0:T(8,128)(2,1)}, u32[]{:S(2)}, u32[]{:S(2)}) collective-permute-start(bf16[8,3,128,128]{3,2,1,0:T(8,128)(2,1)S(1)} %get-tuple-element.329), channel_id=1, source_target_pairs={{1,0},{2,1},{3,2},{4,3},{5,4},{6,5},{7,6},{8,7},{9,8},{10,9},{11,1... | collective-permute-start | bytes 2359304 | tf_op jit(solution)/shard_map/ppermute | solution.py:18
  14.5 3.3 copy-start.8
  35.8 4.3 copy-start
  72.5 3.1 copy-start.3
  75.6 1.5 copy-start.2
  78.6 4.3 copy-start
  115.3 3.1 copy-start.3
  118.4 1.5 copy-start.2
  121.3 4.3 copy-start
  158.1 3.1 copy-start.3
  161.2 1.5 copy-start.2
  164.1 4.3 copy-start
  200.9 3.1 copy-start.3
  207.0 4.3 copy-start
  243.7 3.1 copy-start.3
  249.8 4.3 copy-start
  286.6 3.1 copy-start.3
  292.6 4.3 copy-start
  329.5 3.1 copy-start.3
  335.5 4.3 copy-start
  372.3 3.1 copy-start.3
  378.2 4.3 copy-start
  415.0 3.1 copy-start.3
  421.0 4.3 copy-start
  457.8 3.1 copy-start.3
  477.0 17.5 %copy-start.1 = (f32[7,21,128,128]{3,2,1,0:T(8,128)S(1)}, f32[7,21,128,128]{3,2,1,0:T(8,128)}, u32[]{:S(2)}) copy-start(f32[7,21,128,128]{3,2,1,0:T(8,128)} %copy.25) | copy-start | bytes 28901380
  477.1 17.3 %collective-permute-start.2 = (bf16[21,128,128]{2,1,0:T(8,128)(2,1)S(1)}, bf16[21,128,128]{2,1,0:T(8,128)(2,1)S(1)}, u32[]{:S(2)}, u32[]{:S(2)}) collective-permute-start(bf16[21,128,128]{2,1,0:T(8,128)(2,1)S(1)} %get-tuple-element.327), channel_id=1, source_target_pairs={{0,1},{1,2},{2,3},{3,4},{4,5},{5,6},{6,7},{7,8},{8,9},{9,10},{10,1... | collective-permute-start | bytes 2064392 | tf_op jit(solution)/shard_map/ppermute | solution.py:26
  481.0 13.5 %slice-start = ((f32[7,21,128,128]{3,2,1,0:T(8,128)}), f32[5,21,128,128]{3,2,1,0:T(8,128)S(1)}, s32[]{:S(2)}) async-start(f32[7,21,128,128]{3,2,1,0:T(8,128)} %copy.25), calls=%async_computation | async-start | bytes 13762560 | tf_op jit(solution)/shard_map/slice | solution.py:95
  481.0 18.4 %collective-permute-start.3 = (bf16[21,128,128]{2,1,0:T(8,128)(2,1)S(1)}, bf16[21,128,128]{2,1,0:T(8,128)(2,1)S(1)}, u32[]{:S(2)}, u32[]{:S(2)}) collective-permute-start(bf16[21,128,128]{2,1,0:T(8,128)(2,1)S(1)} %get-tuple-element.326), channel_id=1, source_target_pairs={{1,0},{2,1},{3,2},{4,3},{5,4},{6,5},{7,6},{8,7},{9,8},{10,9},{11,1... | collective-permute-start | bytes 2064392 | tf_op jit(solution)/shard_map/ppermute | solution.py:26
  (9 other events, 12.6 us)
where the time goes:
time: 511 us; the launch traced here: 502 us
  loops' own time  191 us (37%)
  other arithmetic  168 us (33%)
  local copies, waits for them, and re-layouts  52.5 us (10%)
  matrix products  49.6 us (10%)
  starting transfers between devices  22.1 us (4%)
  waiting for transfers between devices  18.8 us (4%)
    another operation x1, loops' own time, coarse_rows(): return lax.fori_loop(0, fp, step, start)  191 us
    dynamic_update_slice x30, other arithmetic, step(): acc = lax.dynamic_update_slice(acc, current + terms[block][None], begin)  89.6 us
    dynamic_update_slice x70, other arithmetic, step(): lax.dynamic_update_slice_in_dim(window, current + prods[slot_k], where, 0)  67.4 us
    dot_general x10, matrix products, step(): jnp.einsum('qba,rbc->qrac', own_p, product, preferred_element_type=jnp.fl...  35.2 us
    dot_general x10, matrix products, step(): jnp.einsum('kab,kqbc->kqac', a_row, picked, preferred_element_type=jnp.fl...  14.4 us
    ppermute x2, waiting for transfers between devices, shifted(): return lax.ppermute(block, axis, route)  11.7 us
    while x2, local copies, waits for them, and re-layouts, coarse_rows(): return lax.fori_loop(0, fp, step, start)  11.3 us
    ppermute x2, starting transfers between devices, shifted(): return lax.ppermute(block, axis, route)  10.3 us
  transfers between devices with their start and end apart: 4, of which 4 were waited for; matrix products, arithmetic and copies ran while one was open for 1% of the time, Pallas kernels for 0%

commit v1 on v0

v1 whole, which is shorter than its diff:
```python
import functools

import jax
import jax.numpy as jnp
from jax import lax
from jax.experimental import pallas as pl
from jax.experimental.pallas import tpu as pltpu
from jax.sharding import PartitionSpec as P

B = 128
FP = 10
CP = 5
KA = 8
REP = 4
NJ = FP + 2 * REP
NT = 17
T0 = -6
KC = 21
MESH = pl.DeviceIdType.MESH


def blk(n, count=1):
    return pl.ds(n * B, count * B)


def dot(x, y):
    return jnp.dot(x, y, preferred_element_type=jnp.float32)


def kernel(
    ndev, nsub,
    cols_s, cnt_s, agg_h, rep_h, a_h, p_h,
    out,
    agg_s, rep_s, p_v, pt_v, a_v, ad, r, ra, pd, pl_own, acc,
    sendp, recvp, sendg, recvg, sendc, recvc,
    meta_sem, load_sem, send_sem, recv_sem,
):
    e = lax.axis_index("rows") * nsub + lax.axis_index("sub")
    up = lax.rem(e + 1, ndev)
    dn = lax.rem(e + ndev - 1, ndev)
    peers = ((dn // nsub, lax.rem(dn, nsub)), (up // nsub, lax.rem(up, nsub)))

    barrier = pltpu.get_barrier_semaphore()
    for peer in peers:
        pl.semaphore_signal(barrier, inc=1, device_id=peer, device_id_type=MESH)

    load_p = pltpu.make_async_copy(p_h, p_v.at[pl.ds(0, 3 * FP)], load_sem.at[0])
    load_p.start()
    meta = []
    for n, d in enumerate((dn, e, up)):
        meta.append(pltpu.make_async_copy(agg_h.at[d], agg_s.at[n], meta_sem.at[n]))
        meta.append(pltpu.make_async_copy(rep_h.at[d], rep_s.at[n], meta_sem.at[3 + n]))
    for copy in meta:
        copy.start()
    load_a = pltpu.make_async_copy(a_h, a_v.at[pl.ds(0, KA * FP)], load_sem.at[1])
    load_a.start()

    zero = jnp.zeros((B, B), jnp.bfloat16)
    p_v[3 * FP] = zero
    pt_v[3 * FP] = zero
    a_v[KA * FP] = zero
    recvp[0, 3 * REP] = zero
    recvp[1, 3 * REP] = zero

    for copy in meta:
        copy.wait()
    load_p.wait()

    def agg(i):
        return agg_s[1, 0, i]

    for i in range(3):
        low = jnp.where((e == 0) & (agg(i) == 0), 3 * FP, 3 * i)
        p_v[3 * i] = p_v[low]
        k = FP - 1 - i
        high = jnp.where((e == ndev - 1) & (agg(k) == CP - 1), 3 * FP, 3 * k + 2)
        p_v[3 * k + 2] = p_v[high]

    for d in range(2):
        for s in range(REP):
            local = rep_s[1, d, s]
            for q in range(3):
                sendp[d, 3 * s + q] = p_v[3 * local + q]

    def remote(d, n, src, dst):
        return pltpu.make_async_remote_copy(
            src_ref=src, dst_ref=dst, send_sem=send_sem.at[d, n], recv_sem=recv_sem.at[d, n],
            device_id=peers[d], device_id_type=MESH,
        )

    send_p = [remote(d, 0, sendp.at[d], recvp.at[d, pl.ds(0, 3 * REP)]) for d in range(2)]
    send_g = [remote(d, 1, sendg.at[d], recvg.at[d]) for d in range(2)]
    send_c = [remote(d, 2, sendc.at[d], recvc.at[d]) for d in range(2)]
    pl.semaphore_wait(barrier, 2)
    for copy in send_p:
        copy.start()

    def transpose(b, carry):
        pt_v[b] = p_v[b].T
        return carry

    lax.fori_loop(0, 3 * FP, transpose, 0)

    def pick(q, first, none):
        return jnp.where((q >= 0) & (q <= 2), first + q, none)

    for i in range(FP):
        for c in range(CP + 2):
            if (c == 0 and i > 2) or (c == CP + 1 and i < FP - 3):
                continue
            r[blk(c), blk(i)] = pt_v[pick(c - agg(i), 3 * i, 3 * FP)]

    ids = []
    for s in range(REP):
        ids.append(rep_s[0, 1, s] - FP)
    for j in range(FP):
        ids.append(j)
    for s in range(REP):
        ids.append(rep_s[2, 0, s] + FP)

    load_a.wait()

    def spread(i, carry):
        held = [jnp.where(k < cnt_s[i], cols_s[i, k] - e * FP, 1 << 20) for k in range(KA)]
        rows = pl.ds(pl.multiple_of(i * B, B), B)
        for j in range(NJ):
            at = KA * FP
            for k in range(KA):
                at = jnp.where(held[k] == ids[j], i * KA + k, at)
            ad[rows, blk(j)] = a_v[at]
        return carry

    lax.fori_loop(0, FP, spread, 0)

    for c, i in ((0, 0), (CP + 1, FP - 3)):
        for n in range(0, NJ, 6):
            ra[blk(c), blk(n, 6)] = dot(r[blk(c), blk(i, 3)], ad[blk(i, 3), blk(n, 6)]).astype(jnp.bfloat16)

    for j in range(FP):
        for t in range(-1, CP + 1):
            pd[blk(REP + j), blk(t - T0)] = p_v[pick(t - agg(j) + 1, 3 * j, 3 * FP)]

    own = blk(REP, FP)
    for d, c, first, t in ((0, 0, 0, -1), (1, CP + 1, REP + FP, 1)):
        for s in range(REP):
            sendg[d, s] = ra[blk(c), blk(first + s)]
        part = dot(ra[blk(c), own], pd[own, blk(t - T0, 5)]).astype(jnp.bfloat16)
        for n in range(5):
            sendg[d, REP + n] = part[:, n * B : (n + 1) * B]

    mid = blk(1, CP)

    def left(n, carry):
        at = pl.ds(pl.multiple_of(n * 2 * B, 2 * B), 2 * B)
        ra[mid, at] = dot(r[mid, :], ad[:, at]).astype(jnp.bfloat16)
        return carry

    lax.fori_loop(0, NJ // 2, left, 0)

    for d in range(2):
        for s in range(REP):
            local = rep_s[1, d, s]
            for t in range(-1, CP + 1):
                pl_own[d, blk(s), blk(t + 1)] = p_v[pick(t - agg(local) + 1, 3 * local, 3 * FP)]

    def emit(t, count, first, panels):
        part = dot(ra[mid, blk(first, panels)], pd[blk(first, panels), blk(t - T0, count)])
        for n in range(count):
            for c in range(CP):
                block = part[c * B : (c + 1) * B, n * B : (n + 1) * B]
                if c in (0, CP - 1):
                    acc[0 if c == 0 else 1, :, blk(t + n - T0)] = block
                else:
                    out[c, t + n - c + 10] = block.astype(jnp.bfloat16)

    emit(1, 3, REP, FP)

    for copy in send_p:
        copy.wait()
    for copy in send_g:
        copy.start()

    for s in range(REP):
        g = agg_s[0, 0, rep_s[0, 1, s]] - CP
        for t in range(-6, 1):
            pd[blk(s), blk(t - T0)] = recvp[1, pick(t - g + 1, 3 * s, 3 * REP)]
        g = agg_s[2, 0, rep_s[2, 0, s]] + CP
        for t in range(4, 11):
            pd[blk(REP + FP + s), blk(t - T0)] = recvp[0, pick(t - g + 1, 3 * s, 3 * REP)]

    last = REP + FP
    part = dot(ra[blk(0), blk(REP, FP + 1)], pd[blk(REP, FP + 1), blk(4 - T0, 2)]).astype(jnp.bfloat16)
    sendc[0, 0] = part[:, :B]
    sendc[0, 1] = part[:, B:]
    sendc[0, 2] = dot(ra[blk(0), blk(last)], pd[blk(last), blk(6 - T0)]).astype(jnp.bfloat16)
    part = dot(ra[blk(CP + 1), blk(REP - 1, FP + 1)], pd[blk(REP - 1, FP + 1), blk(-1 - T0, 2)]).astype(jnp.bfloat16)
    sendc[1, 1] = part[:, :B]
    sendc[1, 2] = part[:, B:]
    sendc[1, 0] = dot(ra[blk(CP + 1), blk(REP - 1)], pd[blk(REP - 1), blk(-2 - T0)]).astype(jnp.bfloat16)
    for copy in send_c:
        copy.start()

    emit(-1, 2, 0, REP + FP)
    emit(4, 2, REP, FP + REP)
    emit(-6, 5, 0, REP)
    emit(6, 5, REP + FP, REP)

    for c in range(CP):
        for m in range(KC):
            low, high = (3 if c == 0 else CP - 1 - c), (17 if c == CP - 1 else KC - 1 - c)
            if not low <= m <= high:
                out[c, m] = zero

    for copy in send_g:
        copy.wait()
    for copy in send_c:
        copy.wait()

    for d, c, n in ((1, 0, 0), (0, CP - 1, 1)):
        factor = jnp.concatenate([recvg[d, s] for s in range(REP)], axis=1)
        extra = dot(factor, pl_own[n])
        for t in range(T0 - 1, T0 + NT + 1):
            m = t - c + 10
            if not 0 <= m < KC:
                continue
            terms = []
            if T0 <= t < T0 + NT:
                terms.append(acc[n, :, blk(t - T0)])
            if -1 <= t <= CP:
                terms.append(extra[:, (t + 1) * B : (t + 2) * B])
            sent = t + CP if d == 1 else t - CP
            early, late = (1, -2) if d == 1 else (-1, 4)
            if early <= sent < early + 5:
                terms.append(recvg[d, REP + sent - early].astype(jnp.float32))
            if late <= sent < late + 3:
                terms.append(recvc[d, sent - late].astype(jnp.float32))
            if terms:
                out[c, m] = functools.reduce(jnp.add, terms).astype(jnp.bfloat16)


def body(ndev, nsub, a_tiles, a_cols, a_count, p_tiles, aggregate, rep_list):
    bf16 = jnp.bfloat16
    vmem = pltpu.VMEM
    return pl.pallas_call(
        functools.partial(kernel, ndev, nsub),
        out_shape=jax.ShapeDtypeStruct((CP, KC, B, B), bf16),
        in_specs=[pl.BlockSpec(memory_space=pltpu.SMEM)] * 2 + [pl.BlockSpec(memory_space=pl.ANY)] * 4,
        out_specs=pl.BlockSpec(memory_space=pltpu.VMEM),
        scratch_shapes=[
            pltpu.SMEM((3, 1, FP), jnp.int32),
            pltpu.SMEM((3, 2, REP), jnp.int32),
            vmem((3 * FP + 1, B, B), bf16),
            vmem((3 * FP + 1, B, B), bf16),
            vmem((KA * FP + 1, B, B), bf16),
            vmem((FP * B, NJ * B), bf16),
            vmem(((CP + 2) * B, FP * B), bf16),
            vmem(((CP + 2) * B, NJ * B), bf16),
            vmem((NJ * B, NT * B), bf16),
            vmem((2, REP * B, 7 * B), bf16),
            vmem((2, B, NT * B), jnp.float32),
            vmem((2, 3 * REP, B, B), bf16),
            vmem((2, 3 * REP + 1, B, B), bf16),
            vmem((2, REP + 5, B, B), bf16),
            vmem((2, REP + 5, B, B), bf16),
            vmem((2, 3, B, B), bf16),
            vmem((2, 3, B, B), bf16),
            pltpu.SemaphoreType.DMA((6,)),
            pltpu.SemaphoreType.DMA((2,)),
            pltpu.SemaphoreType.DMA((2, 3)),
            pltpu.SemaphoreType.DMA((2, 3)),
        ],
        compiler_params=pltpu.CompilerParams(
            collective_id=0, has_side_effects=True, vmem_limit_bytes=56 << 20
        ),
        name="coarse",
    )(
        a_cols,
        a_count,
        aggregate.reshape(ndev, 1, FP),
        rep_list,
        a_tiles.reshape(FP * KA, B, B),
        p_tiles.reshape(FP * 3, B, B),
    )


def solution(mesh):
    in_specs = (
        P(("rows", "sub"), None, None, None),
        P(("rows", "sub"), None),
        P(("rows", "sub")),
        P(("rows", "sub"), None, None, None),
        P(),
        P(),
    )
    out_specs = P(("rows", "sub"), None, None, None)
    run = functools.partial(body, mesh.size, mesh.shape["sub"])
    return jax.shard_map(run, mesh=mesh, in_specs=in_specs, out_specs=out_specs, check_vma=False)
```

time: 511 us -> 40.9 us (0.08)
  the two profiles are of different devices: /device:TPU:6 before, /device:TPU:8 now
where the time goes in v1:
time: 40.9 us; the launch traced here: 40.6 us
  Pallas kernels  32 us (78%)
  local copies, waits for them, and re-layouts  8.6 us (21%)
    pallas_call x1, Pallas kernels, body(): pl.pallas_call(functools.partial(kernel, ndev, nsub), out_shape=jax.Shape...  32 us
    unnamed x4, local copies, waits for them, and re-layouts  8.6 us

profile of v1, /device:TPU:8, one launch (start us, length us, event | category | flops | bytes accessed | tf_op | source)
XLA Modules:
  0.0 40.6 jit_solution(8730539617638910153)
XLA Ops:
  0.0 1.4 %copy.8.cols_s = s32[10,8]{1,0:T(8,128)} copy(s32[10,8]{0,1:T(8,128)} %param.7) | data formatting | bytes 640 | tf_op args[1]
  1.4 1.5 %copy.7 = s32[256,10]{1,0:T(8,128)} copy(s32[256,10]{0,1:T(8,128)} %param.10) | data formatting | bytes 20480 | tf_op args[4]
  2.8 1.5 %copy.9.rep_h = s32[256,2,4]{2,1,0:T(2,128)} copy(s32[256,2,4]{0,2,1:T(4,128)} %param.11) | data formatting | bytes 16384 | tf_op args[5]
  4.4 32.0 %coarse.1 = bf16[5,21,128,128]{3,2,1,0:T(8,128)(2,1)} custom-call(s32[10,8]{1,0:T(8,128)} %copy.8.cols_s, s32[10]{0:T(128)} %cnt_s.1, s32[256,1,10]{2,1,0:T(1,128)} %bitcast.5, s32[256,2,4]{2,1,0:T(2,128)} %copy.9.rep_h, bf16[80,128,128]{2,1,0:T(8,128)(2,1)} %bitcast.3, bf16[30,128,128]{2,1,0:T(8,128)(2,1)} %bitcast.4), custom_call_target="tpu_custom_call" | custom-call | tf_op jit(solution)/shard_map/coarse/pallas_call | solution.py:244
  36.4 4.2 %copy.11 = bf16[5,21,128,128]{3,2,1,0:T(8,128)(2,1)} copy(bf16[5,21,128,128]{3,2,1,0:T(8,128)(2,1)} %coarse.1) | data formatting | bytes 6881280

commit v2 on v1

--- a/solution.py
+++ b/solution.py
@@ -29,45 +29,59 @@
 
 def kernel(
     ndev, nsub,
-    cols_s, cnt_s, agg_h, rep_h, a_h, p_h,
+    cols_h, cnt_h, agg_h, rep_h, a_h, p_h,
     out,
-    agg_s, rep_s, p_v, pt_v, a_v, ad, r, ra, pd, pl_own, acc,
-    sendp, recvp, sendg, recvg, sendc, recvc,
-    meta_sem, load_sem, send_sem, recv_sem,
+    cols_s, cnt_s, agg_s, rep_s, p_v, pt_v, a_v, ad, r, ra, pd, pl_own, acc,
+    sendp, recvp_up, recvp_dn, sendg, recvg, sendc, recvc,
+    load_sem, send_sem, recv_sem, ready_sem,
 ):
     e = lax.axis_index("rows") * nsub + lax.axis_index("sub")
     up = lax.rem(e + 1, ndev)
     dn = lax.rem(e + ndev - 1, ndev)
     peers = ((dn // nsub, lax.rem(dn, nsub)), (up // nsub, lax.rem(up, nsub)))
 
+    has_dn = e > 0
+    has_up = e < ndev - 1
+    sends, receives = (has_dn, has_up), (has_up, has_dn)
+
     barrier = pltpu.get_barrier_semaphore()
-    for peer in peers:
-        pl.semaphore_signal(barrier, inc=1, device_id=peer, device_id_type=MESH)
+
+    @pl.when(has_dn)
+    def _():
+        pl.semaphore_signal(barrier, inc=1, device_id=peers[0], device_id_type=MESH)
 
     load_p = pltpu.make_async_copy(p_h, p_v.at[pl.ds(0, 3 * FP)], load_sem.at[0])
     load_p.start()
-    meta = []
-    for n, d in enumerate((dn, e, up)):
-        meta.append(pltpu.make_async_copy(agg_h.at[d], agg_s.at[n], meta_sem.at[n]))
-        meta.append(pltpu.make_async_copy(rep_h.at[d], rep_s.at[n], meta_sem.at[3 + n]))
+    meta = [
+        pltpu.make_async_copy(src, dst, load_sem.at[2 + n])
+        for n, (src, dst) in enumerate(((rep_h, rep_s), (agg_h, agg_s), (cols_h, cols_s), (cnt_h, cnt_s)))
+    ]
     for copy in meta:
         copy.start()
     load_a = pltpu.make_async_copy(a_h, a_v.at[pl.ds(0, KA * FP)], load_sem.at[1])
     load_a.start()
 
+    recvp = (recvp_up, recvp_dn)
+
     zero = jnp.zeros((B, B), jnp.bfloat16)
     p_v[3 * FP] = zero
     pt_v[3 * FP] = zero
     a_v[KA * FP] = zero
-    recvp[0, 3 * REP] = zero
-    recvp[1, 3 * REP] = zero
+    recvp_up[3 * REP] = zero
+    recvp_dn[3 * REP] = zero
+
+
+    @pl.when(has_up)
+    def _():
+        pl.semaphore_wait(barrier, 1)
+        pl.semaphore_signal(ready_sem, inc=1, device_id=peers[1], device_id_type=MESH)
 
     for copy in meta:
         copy.wait()
     load_p.wait()
 
     def agg(i):
-        return agg_s[1, 0, i]
+        return agg_s[i, e]
 
     for i in range(3):
         low = jnp.where((e == 0) & (agg(i) == 0), 3 * FP, 3 * i)
@@ -76,24 +90,37 @@
         high = jnp.where((e == ndev - 1) & (agg(k) == CP - 1), 3 * FP, 3 * k + 2)
         p_v[3 * k + 2] = p_v[high]
 
-    for d in range(2):
-        for s in range(REP):
-            local = rep_s[1, d, s]
-            for q in range(3):
-                sendp[d, 3 * s + q] = p_v[3 * local + q]
-
     def remote(d, n, src, dst):
         return pltpu.make_async_remote_copy(
             src_ref=src, dst_ref=dst, send_sem=send_sem.at[d, n], recv_sem=recv_sem.at[d, n],
             device_id=peers[d], device_id_type=MESH,
         )
 
-    send_p = [remote(d, 0, sendp.at[d], recvp.at[d, pl.ds(0, 3 * REP)]) for d in range(2)]
+    send_p = [remote(d, 0, sendp.at[d], recvp[d].at[pl.ds(0, 3 * REP)]) for d in range(2)]
     send_g = [remote(d, 1, sendg.at[d], recvg.at[d]) for d in range(2)]
     send_c = [remote(d, 2, sendc.at[d], recvc.at[d]) for d in range(2)]
-    pl.semaphore_wait(barrier, 2)
-    for copy in send_p:
-        copy.start()
+
+    def start(copies, d):
+        pl.when(sends[d])(copies[d].start)
+
+    def arrived(copies, d):
+        pl.when(receives[d])(copies[d].wait_recv)
+
+    for d in (1, 0):
+        for s in range(REP):
+            local = rep_s[d, s, e]
+            for q in range(3):
+                sendp[d, 3 * s + q] = p_v[3 * local + q]
+        if d == 0:
+            pl.when(has_dn)(lambda: pl.semaphore_wait(ready_sem, 1))
+        start(send_p, d)
+
+    for d in range(2):
+        @pl.when(jnp.logical_not(receives[d]))
+        def _():
+            recvp[d][...] = jnp.zeros(recvp[d].shape, jnp.bfloat16)
+            recvg[d] = jnp.zeros(recvg.shape[1:], jnp.bfloat16)
+            recvc[d] = jnp.zeros(recvc.shape[1:], jnp.bfloat16)
 
     def transpose(b, carry):
         pt_v[b] = p_v[b].T
@@ -112,16 +139,16 @@
 
     ids = []
     for s in range(REP):
-        ids.append(rep_s[0, 1, s] - FP)
+        ids.append(rep_s[1, s, dn] - FP)
     for j in range(FP):
         ids.append(j)
     for s in range(REP):
-        ids.append(rep_s[2, 0, s] + FP)
+        ids.append(rep_s[0, s, up] + FP)
 
     load_a.wait()
 
     def spread(i, carry):
-        held = [jnp.where(k < cnt_s[i], cols_s[i, k] - e * FP, 1 << 20) for k in range(KA)]
+        held = [jnp.where(k < cnt_s[0, i], cols_s[k, i] - e * FP, 1 << 20) for k in range(KA)]
         rows = pl.ds(pl.multiple_of(i * B, B), B)
         for j in range(NJ):
             at = KA * FP
@@ -148,6 +175,9 @@
         for n in range(5):
             sendg[d, REP + n] = part[:, n * B : (n + 1) * B]
 
+    for d in (1, 0):
+        start(send_g, d)
+
     mid = blk(1, CP)
 
     def left(n, carry):
@@ -159,7 +189,7 @@
 
     for d in range(2):
         for s in range(REP):
-            local = rep_s[1, d, s]
+            local = rep_s[d, s, e]
             for t in range(-1, CP + 1):
                 pl_own[d, blk(s), blk(t + 1)] = p_v[pick(t - agg(local) + 1, 3 * local, 3 * FP)]
 
@@ -175,35 +205,33 @@
 
     emit(1, 3, REP, FP)
 
-    for copy in send_p:
-        copy.wait()
-    for copy in send_g:
-        copy.start()
-
+    last = REP + FP
+    arrived(send_p, 0)
     for s in range(REP):
-        g = agg_s[0, 0, rep_s[0, 1, s]] - CP
-        for t in range(-6, 1):
-            pd[blk(s), blk(t - T0)] = recvp[1, pick(t - g + 1, 3 * s, 3 * REP)]
-        g = agg_s[2, 0, rep_s[2, 0, s]] + CP
+        g = agg_s[rep_s[0, s, up], up] + CP
         for t in range(4, 11):
-            pd[blk(REP + FP + s), blk(t - T0)] = recvp[0, pick(t - g + 1, 3 * s, 3 * REP)]
-
-    last = REP + FP
+            pd[blk(last + s), blk(t - T0)] = recvp_up[pick(t - g + 1, 3 * s, 3 * REP)]
     part = dot(ra[blk(0), blk(REP, FP + 1)], pd[blk(REP, FP + 1), blk(4 - T0, 2)]).astype(jnp.bfloat16)
     sendc[0, 0] = part[:, :B]
     sendc[0, 1] = part[:, B:]
     sendc[0, 2] = dot(ra[blk(0), blk(last)], pd[blk(last), blk(6 - T0)]).astype(jnp.bfloat16)
+    start(send_c, 0)
+
+    arrived(send_p, 1)
+    for s in range(REP):
+        g = agg_s[rep_s[1, s, dn], dn] - CP
+        for t in range(-6, 1):
+            pd[blk(s), blk(t - T0)] = recvp_dn[pick(t - g + 1, 3 * s, 3 * REP)]
     part = dot(ra[blk(CP + 1), blk(REP - 1, FP + 1)], pd[blk(REP - 1, FP + 1), blk(-1 - T0, 2)]).astype(jnp.bfloat16)
     sendc[1, 1] = part[:, :B]
     sendc[1, 2] = part[:, B:]
     sendc[1, 0] = dot(ra[blk(CP + 1), blk(REP - 1)], pd[blk(REP - 1), blk(-2 - T0)]).astype(jnp.bfloat16)
-    for copy in send_c:
-        copy.start()
-
+    start(send_c, 1)
+
+    emit(4, 2, REP, FP + REP)
+    emit(6, 5, last, REP)
     emit(-1, 2, 0, REP + FP)
-    emit(4, 2, REP, FP + REP)
     emit(-6, 5, 0, REP)
-    emit(6, 5, REP + FP, REP)
 
     for c in range(CP):
         for m in range(KC):
@@ -211,14 +239,12 @@
             if not low <= m <= high:
                 out[c, m] = zero
 
-    for copy in send_g:
-        copy.wait()
-    for copy in send_c:
-        copy.wait()
-
-    for d, c, n in ((1, 0, 0), (0, CP - 1, 1)):
+    for d, c, n in ((0, CP - 1, 1), (1, 0, 0)):
+        arrived(send_g, d)
         factor = jnp.concatenate([recvg[d, s] for s in range(REP)], axis=1)
         extra = dot(factor, pl_own[n])
+        early, late = (1, -2) if d == 1 else (-1, 4)
+        held = {}
         for t in range(T0 - 1, T0 + NT + 1):
             m = t - c + 10
             if not 0 <= m < KC:
@@ -229,13 +255,25 @@
             if -1 <= t <= CP:
                 terms.append(extra[:, (t + 1) * B : (t + 2) * B])
             sent = t + CP if d == 1 else t - CP
-            early, late = (1, -2) if d == 1 else (-1, 4)
             if early <= sent < early + 5:
                 terms.append(recvg[d, REP + sent - early].astype(jnp.float32))
+            total = functools.reduce(jnp.add, terms) if terms else None
             if late <= sent < late + 3:
-                terms.append(recvc[d, sent - late].astype(jnp.float32))
-            if terms:
-                out[c, m] = functools.reduce(jnp.add, terms).astype(jnp.bfloat16)
+                if total is not None:
+                    acc[n, :, blk(t - T0)] = total
+                held[m] = (sent - late, t, total is not None)
+            elif terms:
+                out[c, m] = total.astype(jnp.bfloat16)
+        arrived(send_c, d)
+        for m, (at, t, more) in held.items():
+            total = recvc[d, at].astype(jnp.float32)
+            if more:
+                total = total + acc[n, :, blk(t - T0)]
+            out[c, m] = total.astype(jnp.bfloat16)
+
+    for copies in (send_p, send_g, send_c):
+        for d in range(2):
+            pl.when(sends[d])(copies[d].wait_send)
 
 
 def body(ndev, nsub, a_tiles, a_cols, a_count, p_tiles, aggregate, rep_list):
@@ -243,12 +281,14 @@
     vmem = pltpu.VMEM
     return pl.pallas_call(
         functools.partial(kernel, ndev, nsub),
-        out_shape=jax.ShapeDtypeStruct((CP, KC, B, B), bf16),
-        in_specs=[pl.BlockSpec(memory_space=pltpu.SMEM)] * 2 + [pl.BlockSpec(memory_space=pl.ANY)] * 4,
+        out_shape=pltpu.VMEM((CP, KC, B, B), bf16),
+        in_specs=[pl.BlockSpec(memory_space=pl.ANY)] * 6,
         out_specs=pl.BlockSpec(memory_space=pltpu.VMEM),
         scratch_shapes=[
-            pltpu.SMEM((3, 1, FP), jnp.int32),
-            pltpu.SMEM((3, 2, REP), jnp.int32),
+            pltpu.SMEM((KA, FP), jnp.int32),
+            pltpu.SMEM((1, FP), jnp.int32),
+            pltpu.SMEM((FP, ndev), jnp.int32),
+            pltpu.SMEM((2, REP, ndev), jnp.int32),
             vmem((3 * FP + 1, B, B), bf16),
             vmem((3 * FP + 1, B, B), bf16),
             vmem((KA * FP + 1, B, B), bf16),
@@ -259,25 +299,26 @@
             vmem((2, REP * B, 7 * B), bf16),
             vmem((2, B, NT * B), jnp.float32),
             vmem((2, 3 * REP, B, B), bf16),
-            vmem((2, 3 * REP + 1, B, B), bf16),
+            vmem((3 * REP + 1, B, B), bf16),
+            vmem((3 * REP + 1, B, B), bf16),
             vmem((2, REP + 5, B, B), bf16),
             vmem((2, REP + 5, B, B), bf16),
             vmem((2, 3, B, B), bf16),
             vmem((2, 3, B, B), bf16),
             pltpu.SemaphoreType.DMA((6,)),
-            pltpu.SemaphoreType.DMA((2,)),
             pltpu.SemaphoreType.DMA((2, 3)),
             pltpu.SemaphoreType.DMA((2, 3)),
+            pltpu.SemaphoreType.REGULAR,
         ],
         compiler_params=pltpu.CompilerParams(
             collective_id=0, has_side_effects=True, vmem_limit_bytes=56 << 20
         ),
         name="coarse",
     )(
-        a_cols,
-        a_count,
-        aggregate.reshape(ndev, 1, FP),
-        rep_list,
+        a_cols.T,
+        a_count.reshape(1, FP),
+        aggregate.T,
+        rep_list.transpose(1, 2, 0),
         a_tiles.reshape(FP * KA, B, B),
         p_tiles.reshape(FP * 3, B, B),
     )

time: 40.9 us -> 27.4 us (0.67)
  the two profiles are of different devices: /device:TPU:8 before, /device:TPU:6 now
where the time goes in v2:
time: 27.4 us; the launch traced here: 27.3 us
  Pallas kernels  25.6 us (93%)
  local copies, waits for them, and re-layouts  1.76 us (6%)
    pallas_call x1, Pallas kernels, body(): pl.pallas_call(functools.partial(kernel, ndev, nsub), out_shape=pltpu.VME...  25.6 us
    unnamed x1, local copies, waits for them, and re-layouts  1.76 us

profile of v2, /device:TPU:6, one launch (start us, length us, event | category | flops | bytes accessed | tf_op | source)
XLA Modules:
  0.0 27.3 jit_solution(6210339366306147623)
XLA Ops:
  0.0 25.6 %coarse.1 = bf16[5,21,128,128]{3,2,1,0:T(8,128)(2,1)S(1)} custom-call(s32[8,10]{1,0:T(8,128)} %bitcast.10, s32[1,10]{1,0:T(1,128)} %bitcast.11, s32[10,256]{1,0:T(8,128)} %bitcast.8, s32[2,4,256]{2,1,0:T(4,128)} %bitcast.9, bf16[80,128,128]{2,1,0:T(8,128)(2,1)} %bitcast.6, bf16[30,128,128]{2,1,0:T(8,128)(2,1)} %bitcast.7), custom_call_target="tpu_custom_call" | custom-call | tf_op jit(solution)/shard_map/coarse/pallas_call | solution.py:282
  25.6 1.8 %copy.8 = bf16[5,21,128,128]{3,2,1,0:T(8,128)(2,1)} copy(bf16[5,21,128,128]{3,2,1,0:T(8,128)(2,1)S(1)} %coarse.1) | data formatting | bytes 6881280

commit v3 on v2

--- a/solution.py
+++ b/solution.py
@@ -15,6 +15,7 @@
 NJ = FP + 2 * REP
 NT = 17
 T0 = -6
+ROWS_X = 16
 KC = 21
 MESH = pl.DeviceIdType.MESH
 
@@ -59,10 +60,10 @@
     for copy in meta:
         copy.start()
     load_a = pltpu.make_async_copy(a_h, a_v.at[pl.ds(0, KA * FP)], load_sem.at[1])
+
+    recvp = (recvp_up, recvp_dn)
+
     load_a.start()
-
-    recvp = (recvp_up, recvp_dn)
-
     zero = jnp.zeros((B, B), jnp.bfloat16)
     p_v[3 * FP] = zero
     pt_v[3 * FP] = zero
@@ -111,9 +112,15 @@
             local = rep_s[d, s, e]
             for q in range(3):
                 sendp[d, 3 * s + q] = p_v[3 * local + q]
-        if d == 0:
-            pl.when(has_dn)(lambda: pl.semaphore_wait(ready_sem, 1))
-        start(send_p, d)
+        if d == 1:
+            start(send_p, d)
+
+    def start_down():
+        pl.semaphore_wait(ready_sem, 1)
+        send_p[0].start()
+
+    ahead = lax.rem(e, nsub * ROWS_X) == 0
+    pl.when(has_dn & jnp.logical_not(ahead))(start_down)
 
     for d in range(2):
         @pl.when(jnp.logical_not(receives[d]))
@@ -175,6 +182,7 @@
         for n in range(5):
             sendg[d, REP + n] = part[:, n * B : (n + 1) * B]
 
+    pl.when(has_dn & ahead)(start_down)
     for d in (1, 0):
         start(send_g, d)
 
@@ -186,12 +194,6 @@
         return carry
 
     lax.fori_loop(0, NJ // 2, left, 0)
-
-    for d in range(2):
-        for s in range(REP):
-            local = rep_s[d, s, e]
-            for t in range(-1, CP + 1):
-                pl_own[d, blk(s), blk(t + 1)] = p_v[pick(t - agg(local) + 1, 3 * local, 3 * FP)]
 
     def emit(t, count, first, panels):
         part = dot(ra[mid, blk(first, panels)], pd[blk(first, panels), blk(t - T0, count)])
@@ -202,8 +204,6 @@
                     acc[0 if c == 0 else 1, :, blk(t + n - T0)] = block
                 else:
                     out[c, t + n - c + 10] = block.astype(jnp.bfloat16)
-
-    emit(1, 3, REP, FP)
 
     last = REP + FP
     arrived(send_p, 0)
@@ -228,10 +228,17 @@
     sendc[1, 0] = dot(ra[blk(CP + 1), blk(REP - 1)], pd[blk(REP - 1), blk(-2 - T0)]).astype(jnp.bfloat16)
     start(send_c, 1)
 
+    emit(1, 3, REP, FP)
     emit(4, 2, REP, FP + REP)
     emit(6, 5, last, REP)
     emit(-1, 2, 0, REP + FP)
     emit(-6, 5, 0, REP)
+
+    for d in range(2):
+        for s in range(REP):
+            local = rep_s[d, s, e]
+            for t in range(-1, CP + 1):
+                pl_own[d, blk(s), blk(t + 1)] = p_v[pick(t - agg(local) + 1, 3 * local, 3 * FP)]
 
     for c in range(CP):
         for m in range(KC):

time: 27.4 us -> 26.3 us (0.960)
  Pallas kernels: 25.6 us -> 24.4 us
    pallas_call x1, Pallas kernels: 25.6 us -> 24.4 us  [body(): pl.pallas_call(functools.partial(kernel, ndev, nsub), out_shape=pltpu.VME...]
where the time goes in v3:
time: 26.3 us; the launch traced here: 26.2 us
  Pallas kernels  24.4 us (93%)
  local copies, waits for them, and re-layouts  1.76 us (7%)
    pallas_call x1, Pallas kernels, body(): pl.pallas_call(functools.partial(kernel, ndev, nsub), out_shape=pltpu.VME...  24.4 us
    unnamed x1, local copies, waits for them, and re-layouts  1.76 us

profile of v3, /device:TPU:6, one launch (start us, length us, event | category | flops | bytes accessed | tf_op | source)
XLA Modules:
  0.0 26.2 jit_solution(4025604614042087464)
XLA Ops:
  0.0 24.4 %coarse.1 = bf16[5,21,128,128]{3,2,1,0:T(8,128)(2,1)S(1)} custom-call(s32[8,10]{1,0:T(8,128)} %bitcast.10, s32[1,10]{1,0:T(1,128)} %bitcast.11, s32[10,256]{1,0:T(8,128)} %bitcast.8, s32[2,4,256]{2,1,0:T(4,128)} %bitcast.9, bf16[80,128,128]{2,1,0:T(8,128)(2,1)} %bitcast.6, bf16[30,128,128]{2,1,0:T(8,128)(2,1)} %bitcast.7), custom_call_target="tpu_custom_call" | custom-call | tf_op jit(solution)/shard_map/coarse/pallas_call | solution.py:289
  24.4 1.8 %copy.8 = bf16[5,21,128,128]{3,2,1,0:T(8,128)(2,1)} copy(bf16[5,21,128,128]{3,2,1,0:T(8,128)(2,1)S(1)} %coarse.1) | data formatting | bytes 6881280

commit v4 on v3

--- a/solution.py
+++ b/solution.py
@@ -193,7 +193,7 @@
         ra[mid, at] = dot(r[mid, :], ad[:, at]).astype(jnp.bfloat16)
         return carry
 
-    lax.fori_loop(0, NJ // 2, left, 0)
+    lax.fori_loop(0, NJ // 2, left, 0, unroll=3)
 
     def emit(t, count, first, panels):
         part = dot(ra[mid, blk(first, panels)], pd[blk(first, panels), blk(t - T0, count)])
@@ -206,6 +206,17 @@
                     out[c, t + n - c + 10] = block.astype(jnp.bfloat16)
 
     last = REP + FP
+    arrived(send_p, 1)
+    for s in range(REP):
+        g = agg_s[rep_s[1, s, dn], dn] - CP
+        for t in range(-6, 1):
+            pd[blk(s), blk(t - T0)] = recvp_dn[pick(t - g + 1, 3 * s, 3 * REP)]
+    part = dot(ra[blk(CP + 1), blk(REP - 1, FP + 1)], pd[blk(REP - 1, FP + 1), blk(-1 - T0, 2)]).astype(jnp.bfloat16)
+    sendc[1, 1] = part[:, :B]
+    sendc[1, 2] = part[:, B:]
+    sendc[1, 0] = dot(ra[blk(CP + 1), blk(REP - 1)], pd[blk(REP - 1), blk(-2 - T0)]).astype(jnp.bfloat16)
+    start(send_c, 1)
+
     arrived(send_p, 0)
     for s in range(REP):
         g = agg_s[rep_s[0, s, up], up] + CP
@@ -216,17 +227,6 @@
     sendc[0, 1] = part[:, B:]
     sendc[0, 2] = dot(ra[blk(0), blk(last)], pd[blk(last), blk(6 - T0)]).astype(jnp.bfloat16)
     start(send_c, 0)
-
-    arrived(send_p, 1)
-    for s in range(REP):
-        g = agg_s[rep_s[1, s, dn], dn] - CP
-        for t in range(-6, 1):
-            pd[blk(s), blk(t - T0)] = recvp_dn[pick(t - g + 1, 3 * s, 3 * REP)]
-    part = dot(ra[blk(CP + 1), blk(REP - 1, FP + 1)], pd[blk(REP - 1, FP + 1), blk(-1 - T0, 2)]).astype(jnp.bfloat16)
-    sendc[1, 1] = part[:, :B]
-    sendc[1, 2] = part[:, B:]
-    sendc[1, 0] = dot(ra[blk(CP + 1), blk(REP - 1)], pd[blk(REP - 1), blk(-2 - T0)]).astype(jnp.bfloat16)
-    start(send_c, 1)
 
     emit(1, 3, REP, FP)
     emit(4, 2, REP, FP + REP)

time: 26.3 us -> 25.3 us (0.962); the launches traced: 26.2 us -> 24.9 us
  Pallas kernels: 24.4 us -> 23.1 us
    pallas_call x1, Pallas kernels: 24.4 us -> 23.1 us  [body(): pl.pallas_call(functools.partial(kernel, ndev, nsub), out_shape=pltpu.VME...]
where the time goes in v4:
time: 25.3 us; the launch traced here: 24.9 us
  Pallas kernels  23.1 us (91%)
  local copies, waits for them, and re-layouts  1.76 us (7%)
    pallas_call x1, Pallas kernels, body(): pl.pallas_call(functools.partial(kernel, ndev, nsub), out_shape=pltpu.VME...  23.1 us
    unnamed x1, local copies, waits for them, and re-layouts  1.76 us

profile of v4, /device:TPU:6, one launch (start us, length us, event | category | flops | bytes accessed | tf_op | source)
XLA Modules:
  0.0 24.9 jit_solution(9455345206893794168)
XLA Ops:
  0.0 23.1 %coarse.1 = bf16[5,21,128,128]{3,2,1,0:T(8,128)(2,1)S(1)} custom-call(s32[8,10]{1,0:T(8,128)} %bitcast.10, s32[1,10]{1,0:T(1,128)} %bitcast.11, s32[10,256]{1,0:T(8,128)} %bitcast.8, s32[2,4,256]{2,1,0:T(4,128)} %bitcast.9, bf16[80,128,128]{2,1,0:T(8,128)(2,1)} %bitcast.6, bf16[30,128,128]{2,1,0:T(8,128)(2,1)} %bitcast.7), custom_call_target="tpu_custom_call" | custom-call | tf_op jit(solution)/shard_map/coarse/pallas_call | solution.py:289
  23.1 1.8 %copy.8 = bf16[5,21,128,128]{3,2,1,0:T(8,128)(2,1)} copy(bf16[5,21,128,128]{3,2,1,0:T(8,128)(2,1)S(1)} %coarse.1) | data formatting | bytes 6881280

commit v5 on v4

--- a/solution.py
+++ b/solution.py
@@ -183,8 +183,6 @@
             sendg[d, REP + n] = part[:, n * B : (n + 1) * B]
 
     pl.when(has_dn & ahead)(start_down)
-    for d in (1, 0):
-        start(send_g, d)
 
     mid = blk(1, CP)
 
@@ -193,7 +191,10 @@
         ra[mid, at] = dot(r[mid, :], ad[:, at]).astype(jnp.bfloat16)
         return carry
 
-    lax.fori_loop(0, NJ // 2, left, 0, unroll=3)
+    lax.fori_loop(0, 3, left, 0, unroll=3)
+    for d in (1, 0):
+        start(send_g, d)
+    lax.fori_loop(3, NJ // 2, left, 0, unroll=3)
 
     def emit(t, count, first, panels):
         part = dot(ra[mid, blk(first, panels)], pd[blk(first, panels), blk(t - T0, count)])

time: 25.3 us -> 25.3 us (level)
  no operation moved by 1% of the time
where the time goes in v5:
time: 25.3 us; the launch traced here: 24.8 us
  Pallas kernels  23.1 us (91%)
  local copies, waits for them, and re-layouts  1.76 us (7%)
    pallas_call x1, Pallas kernels, body(): pl.pallas_call(functools.partial(kernel, ndev, nsub), out_shape=pltpu.VME...  23.1 us
    unnamed x1, local copies, waits for them, and re-layouts  1.76 us

profile of v5, /device:TPU:6, one launch (start us, length us, event | category | flops | bytes accessed | tf_op | source)
XLA Modules:
  0.0 24.8 jit_solution(7332455043105640551)
XLA Ops:
  0.0 23.1 %coarse.1 = bf16[5,21,128,128]{3,2,1,0:T(8,128)(2,1)S(1)} custom-call(s32[8,10]{1,0:T(8,128)} %bitcast.10, s32[1,10]{1,0:T(1,128)} %bitcast.11, s32[10,256]{1,0:T(8,128)} %bitcast.8, s32[2,4,256]{2,1,0:T(4,128)} %bitcast.9, bf16[80,128,128]{2,1,0:T(8,128)(2,1)} %bitcast.6, bf16[30,128,128]{2,1,0:T(8,128)(2,1)} %bitcast.7), custom_call_target="tpu_custom_call" | custom-call | tf_op jit(solution)/shard_map/coarse/pallas_call | solution.py:290
  23.1 1.8 %copy.8 = bf16[5,21,128,128]{3,2,1,0:T(8,128)(2,1)} copy(bf16[5,21,128,128]{3,2,1,0:T(8,128)(2,1)S(1)} %coarse.1) | data formatting | bytes 6881280
